TPU v7x, 32 devices: a whole 2x2x4 slice. The times are simulated.
32 devices in a mesh: chain: 4 (over z), param: 8 (over y, x, core).
Axes of the slice: x: 2, y: 2, z: 4, core: 2. Of those that a mesh axis runs over, the one named last changes fastest.
Arguments:
- spins: int32 [128, 256, 4], P(('chain', 'param')), may hold values from 0 to 1
- local_energy: float32 [128], replicated, may hold values from -24 to 24
- embed_weight: float32 [4, 256], replicated, may hold values from -3 to 3
- position: bfloat16 [256, 256], replicated, may hold values from -6 to 6
- value_weight: bfloat16 [256, 256], replicated, may hold values from -0.375 to 0.375
- mixing: bfloat16 [8, 256, 256], replicated, may hold values from -0.375 to 0.375
- out_weight: bfloat16 [256, 256], replicated, may hold values from -0.375 to 0.375
- up_weight: bfloat16 [256, 1024], replicated, may hold values from -0.375 to 0.375
- down_weight: bfloat16 [1024, 256], replicated, may hold values from -0.1875 to 0.1875
- readout: float32 [256], replicated, may hold values from -6 to 6
Outputs:
- up_update: float32 [256, 1024], P('chain', 'param')
- down_update: float32 [1024, 256], P('param', 'chain')
- sample_weights: float32 [128], replicated
All inputs are finite; a program needn't handle non-finite values.
Results may differ from a plain program's by a relative error of at most 0.018.
Values may be sent and summed in bfloat16 or wider, within the bound.
A program may use at most 128 MiB of HBM per device.

v0:
```python
import math
import jax
import jax.numpy as jnp
from jax import lax
from jax.sharding import PartitionSpec as P

damping = 0.05


def layer_norm(hidden_state):
    average = jnp.mean(hidden_state, axis=-1, keepdims=True)
    centred = hidden_state - average
    spread = jnp.mean(centred * centred, axis=-1, keepdims=True)
    return centred * lax.rsqrt(spread + 1e-05)


def project(operand, weights):
    return lax.dot_general(
        operand,
        weights,
        (((operand.ndim - 1,), (0,)), ((), ())),
        preferred_element_type=jnp.float32,
    )


def center_rows(jacobian, total):
    jac_wide = jacobian.astype(jnp.float32)
    return (jac_wide - jnp.mean(jac_wide, axis=0)) / math.sqrt(total)


def gram_of(centred, total):
    flat = centred.reshape(total, -1)
    return lax.dot_general(
        flat,
        flat,
        (((1,), (1,)), ((), ())),
        precision=lax.Precision.HIGHEST,
        preferred_element_type=jnp.float32,
    )


def solve_weights(gram, local_energy, total):
    scale = jnp.trace(gram) / total
    system = gram + damping * scale * jnp.eye(total, dtype=jnp.float32)
    lower = jnp.linalg.cholesky(system)
    energy = (local_energy - jnp.mean(local_energy)) / math.sqrt(total)
    column = energy[:, None]
    middle = lax.linalg.triangular_solve(lower, column, left_side=True, lower=True)
    answer = lax.linalg.triangular_solve(
        lower, middle, left_side=True, lower=True, transpose_a=True
    )
    return scale * answer[:, 0]


def body(
    spins,
    local_energy,
    embed_weight,
    position,
    value_weight,
    mixing,
    out_weight,
    up_weight,
    down_weight,
    readout,
):
    samples = spins.shape[0]
    patch_rows = spins.shape[1]
    total = local_energy.shape[0]
    head_count = mixing.shape[0]
    model_width = value_weight.shape[0]
    spin_values = (2 * spins - 1).astype(jnp.float32)
    embedded = jnp.sum(spin_values[..., None] * embed_weight, axis=2) + position.astype(jnp.float32)
    normed = layer_norm(embedded).astype(jnp.bfloat16)
    values = project(normed, value_weight).astype(jnp.bfloat16)
    split_values = values.reshape(samples, patch_rows, head_count, model_width // head_count)
    mixture = jnp.einsum("htu,suhe->sthe", mixing, split_values, preferred_element_type=jnp.float32)
    mixture = mixture.astype(jnp.bfloat16).reshape(samples, patch_rows, model_width)
    residual = embedded + project(mixture, out_weight)
    features = layer_norm(residual).astype(jnp.bfloat16)
    preact = project(features, up_weight)
    hidden = jax.nn.gelu(preact).astype(jnp.bfloat16)
    output = residual + project(hidden, down_weight)
    cotangent = (readout * jnp.tanh(output)).astype(jnp.bfloat16)
    backward = lax.dot_general(
        cotangent, down_weight, (((2,), (1,)), ((), ())), preferred_element_type=jnp.float32
    )
    preact_grad = jax.vjp(jax.nn.gelu, preact)[1](backward)[0].astype(jnp.bfloat16)
    up_block = jnp.einsum("sti,stj->sij", features, preact_grad, preferred_element_type=jnp.float32)
    down_block = jnp.einsum("std,stj->sdj", cotangent, hidden, preferred_element_type=jnp.float32)
    jacobian = jnp.stack([up_block, down_block], axis=1).astype(jnp.bfloat16)
    grouped = lax.all_to_all(jacobian, "param", split_axis=3, concat_axis=0, tiled=True)
    chosen_raw = lax.all_to_all(grouped, "chain", split_axis=2, concat_axis=0, tiled=True)
    centred = center_rows(chosen_raw, total)
    gram = lax.psum(gram_of(centred, total), ("chain", "param"))
    sample_weights = solve_weights(gram, local_energy, total)
    update = -lax.dot_general(
        sample_weights,
        centred,
        (((0,), (0,)), ((), ())),
        precision=lax.Precision.HIGHEST,
        preferred_element_type=jnp.float32,
    )
    return (update[0], update[1].T, sample_weights)


def solution(mesh):
    in_specs = (P(("chain", "param"), None, None), P(), P(), P(), P(), P(), P(), P(), P(), P())
    out_specs = (P("chain", "param"), P("param", "chain"), P())
    return jax.shard_map(body, mesh=mesh, in_specs=in_specs, out_specs=out_specs, check_vma=False)
```

profile of v0, /device:TPU:1, one launch (start us, length us, event | category | flops | bytes accessed | tf_op | source)
XLA Modules:
  0.0 412.8 jit_solution(4878717197872433788)
XLA Ops:
  7.2 0.0 copy-start
  7.2 0.0 all-reduce.2.cloned.1.call-start
  7.2 0.8 add_convert_fusion
  8.1 1.5 multiply_reduce_fusion
  9.5 0.3 copy.91
  9.9 0.0 copy-start.5
  9.9 1.0 copy.90
  10.9 0.1 add_reduce_fusion
  11.0 0.2 multiply_reduce_fusion.2
  11.2 0.0 copy-start.4
  11.2 0.4 convolution_convert_fusion
  11.6 0.5 fusion.17
  12.1 0.0 copy-start.9
  12.2 0.4 fusion.51
  12.5 0.1 multiply_reduce_fusion.1
  12.7 0.8 fusion.26
  13.5 1.9 copy-done.3
  15.4 2.5 fusion.16
  17.9 6.1 %convert_bitcast_fusion.2 = bf16[4,1,256,1024]{3,2,0,1:T(8,128)(2,1)S(1)} fusion(f32[4,256,1024]{2,1,0:T(8,128)} %copy-done.3, bf16[4,256,256]{1,2,0:T(8,128)(2,1)} %fusion.16, bf16[1024,256]{1,0:T(8,128)(2,1)} %param.18, f32[4,256,256]{1,2,0:T(8,128)S(1)} %get-tuple-element.6, f32[4,256]{1,0:T(4,128)S(1)} %add_rsqrt_fusion, ...), kind=kOutput, calls=%fused_computation.21 | convolution fusion | flops 1096548352 | bytes 8396800 | tf_op jit(solution)/shard_map/sti,stj->sij/dot_general | solution.py:89
  24.0 4.1 convert_bitcast_fusion.1
  28.1 2.3 pad_maximum_fusion
  30.4 7.8 %copy.101 = bf16[4,2,256,1024]{2,0,1,3:T(4,128)(2,1)} copy(bf16[4,2,256,1024]{3,2,0,1:T(8,128)(2,1)} %pad_maximum_fusion) | data formatting | bytes 8388608 | tf_op jit(solution)/shard_map/stack | solution.py:91
  38.2 53.2 %all_to_all.27 = bf16[4,2,256,1024]{2,0,1,3:T(4,128)(2,1)S(1)} all-to-all(bf16[4,2,256,1024]{2,0,1,3:T(4,128)(2,1)} %copy.101), channel_id=1, replica_groups=mesh['chain'=4,'param'=8] {'param'}, dimensions={3} | all-to-all | bytes 8388608 | tf_op jit(solution)/shard_map/all_to_all | solution.py:92
  91.4 2.8 copy.102
  94.2 6.5 %copy.103 = bf16[8,4,2,256,128]{4,3,2,1,0:T(8,128)(2,1)} copy(bf16[8,4,2,256,128]{3,4,0,2,1:T(8,128)(2,1)} %bitcast.90) | data formatting | bytes 8388608 | tf_op jit(solution)/shard_map/all_to_all | solution.py:92
  100.6 6.5 %copy.104 = bf16[32,2,256,128]{3,1,0,2:T(2,128)(2,1)S(1)} copy(bf16[32,2,256,128]{3,2,1,0:T(8,128)(2,1)} %bitcast.91) | data formatting | bytes 8388608 | tf_op jit(solution)/shard_map/all_to_all | solution.py:92
  107.2 96.8 %all_to_all.28 = bf16[32,2,256,128]{3,1,0,2:T(2,128)(2,1)S(1)} all-to-all(bf16[32,2,256,128]{3,1,0,2:T(2,128)(2,1)S(1)} %copy.104), channel_id=1, replica_groups=mesh['chain'=4,'param'=8] {'chain'}, dimensions={2} | all-to-all | bytes 8388608 | tf_op jit(solution)/shard_map/all_to_all | solution.py:93
  203.9 4.9 %copy.105 = bf16[32,2,256,128]{3,2,1,0:T(8,128)(2,1)S(1)} copy(bf16[32,2,256,128]{3,1,0,2:T(2,128)(2,1)S(1)} %all_to_all.28) | data formatting | bytes 8388608 | tf_op jit(solution)/shard_map/all_to_all | solution.py:93
  208.8 0.8 fusion.1
  209.6 5.4 %fusion.2 = f32[4,32,2,64,128]{4,3,0,2,1:T(8,128)S(1)} fusion(f32[2,64,128]{2,1,0:T(8,128)S(1)} %broadcast_multiply_fusion, bf16[32,2,256,128]{3,1,0,2:T(2,128)(2,1)S(1)} %all_to_all.28), kind=kLoop, calls=%fused_computation.3 | loop fusion | flops 6291456 | bytes 12648448 | tf_op jit(solution)/shard_map/div | solution.py:28
  215.0 10.4 %copy.106 = f32[4,32,2,64,128]{4,3,2,1,0:T(8,128)S(1)} copy(f32[4,32,2,64,128]{4,3,0,2,1:T(8,128)S(1)} %fusion.2) | data formatting | bytes 16777216 | tf_op jit(solution)/shard_map/div | solution.py:28
  225.4 3.2 copy-done.2
  228.7 17.1 %fusion.18 = f32[128,128]{1,0:T(8,128)} fusion(f32[128,2,64,128]{3,2,1,0:T(8,128)S(1)} %bitcast.88), kind=kOutput, calls=%fused_computation.30 | convolution fusion | flops 3221225472 | bytes 8454144 | tf_op jit(solution)/shard_map/dot_general | solution.py:33
  245.8 0.0 all-reduce.2.cloned.1.call-update
  245.8 0.6 reduce_sum.80
  247.1 117.5 %all-reduce.2.cloned.1.call-done = f32[128,128]{1,0:T(8,128)} async-done(((f32[128,128]{1,0:T(8,128)}), f32[128,128]{1,0:T(8,128)}) %all-reduce.2.cloned.1.call-update) | async-done | bytes 65552 | tf_op jit(solution)/shard_map/psum | solution.py:95
  364.5 1.5 select_reduce_fusion.1
  367.3 0.9 select_add_fusion
  368.1 0.1 copy.109
  368.2 0.9 fusion.37
  369.1 11.7 %cholesky.13 = f32[128,128]{1,0:T(8,128)S(1)} custom-call(f32[128,128]{1,0:T(8,128)S(1)} %fusion.37), custom_call_target="Cholesky" | custom-call | tf_op jit(solution)/shard_map/jit(cholesky)/cholesky | solution.py:45
  380.8 0.6 compare_reduce_fusion
  381.5 0.7 fusion.34
  382.1 9.8 %custom-call.8 = f32[1,128,128]{1,2,0:T(8,128)S(1)} custom-call(f32[1,128,128]{2,1,0:T(8,128)S(1)} %fusion.34), custom_call_target="InvertDiagBlocksLowerTriangular" | custom-call | tf_op jit(solution)/shard_map/triangular_solve | solution.py:49
  392.0 0.2 convolution_bitcast_fusion.1
  392.1 0.2 fusion.21
  392.3 12.5 %fusion.3 = f32[1,2,64,128]{3,0,2,1:T(1,128)S(1)} fusion(f32[128,2,64,128]{3,2,1,0:T(8,128)} %bitcast.89, f32[128]{0:T(128)S(1)} %fusion.21), kind=kOutput, calls=%fused_computation.4 | convolution fusion | flops 25165824 | bytes 8454656 | tf_op jit(solution)/shard_map/dot_general | solution.py:97
  404.9 0.6 slice_bitcast_fusion
  (24 shorter events, 0.1 us)
Async XLA Ops:
  7.2 4.4 %copy-start = (bf16[8,256,256]{2,1,0:T(8,128)(2,1)S(1)}, bf16[8,256,256]{2,1,0:T(8,128)(2,1)}, u32[]{:S(2)}) copy-start(bf16[8,256,256]{2,1,0:T(8,128)(2,1)} %param.15) | copy-start | bytes 3145732
  7.2 4.0 copy-start.6
  7.2 357.3 %all-reduce.2.cloned.1.call-start = ((), (), s32[]{:S(2)}) async-start(), calls=%async_computation.2 | async-start | bytes 131072 | tf_op jit(solution)/shard_map/psum | solution.py:95
  9.9 2.3 copy-start.5
  11.2 1.5 copy-start.4
  12.1 3.2 copy-start.9
  12.2 3.2 copy-start.10
  13.4 1.9 copy-start.3
  225.4 3.2 copy-start.2
  228.7 17.1 %copy-start.8 = (f32[128]{0:T(128)S(1)}, f32[128]{0:T(128)}, u32[]{:S(2)}) copy-start(f32[128]{0:T(128)} %param.11) | copy-start | bytes 1540
  392.1 13.4 %copy-start.1 = (bf16[8,256,256]{2,1,0:T(8,128)(2,1)S(1)}, bf16[8,256,256]{2,1,0:T(8,128)(2,1)}, u32[]{:S(2)}) copy-start(bf16[8,256,256]{2,1,0:T(8,128)(2,1)} %param.15) | copy-start | bytes 3145732
  392.3 12.5 %copy-start.7 = (f32[128]{0:T(128)}, f32[128]{0:T(128)S(1)}, u32[]{:S(2)}) copy-start(f32[128]{0:T(128)S(1)} %fusion.21) | copy-start | bytes 1540
Sparse Core Ops, SparseCore 0:
  245.9 118.5 all-reduce.1
where the time goes:
time: 421 us; the launch traced here: 413 us
  blocking collectives  150 us (36%)
  waiting for transfers between devices  117 us (28%)
  local copies, waits for them, and re-layouts  46.1 us (11%)
  matrix products  44.6 us (11%)
  other arithmetic  37.8 us (9%)
  between operations  16.7 us (4%)
    psum x1, waiting for transfers between devices, body(): gram = lax.psum(gram_of(centred, total), ('chain', 'param'))  117 us
    all_to_all x1, blocking collectives, body(): lax.all_to_all(grouped, 'chain', split_axis=2, concat_axis=0, tiled=True)  96.8 us
    all_to_all x1, blocking collectives, body(): lax.all_to_all(jacobian, 'param', split_axis=3, concat_axis=0, tiled=True)  53.2 us
    dot_general x1, matrix products, gram_of(): lax.dot_general(flat, flat, (((1,), (1,)), ((), ())), precision=lax.Preci...  17.1 us
    all_to_all x3, local copies, waits for them, and re-layouts, body(): lax.all_to_all(jacobian, 'param', split_axis=3, concat_axis=0, tiled=True)  15.7 us
    dot_general x1, matrix products, body(): lax.dot_general(sample_weights, centred, (((0,), (0,)), ((), ())), precis...  12.5 us
    another operation x3, other arithmetic, solve_weights(): lower = jnp.linalg.cholesky(system)  12.4 us
    another operation x2, other arithmetic, solve_weights(): lax.linalg.triangular_solve(lower, middle, left_side=True, lower=True, tr...  10.5 us
  transfers between devices with their start and end apart: 1, of which 1 were waited for; matrix products, arithmetic and copies ran while one was open for 0% of the time, Pallas kernels for 0%

commit v1 on v0

--- a/solution.py
+++ b/solution.py
@@ -89,7 +89,15 @@
     up_block = jnp.einsum("sti,stj->sij", features, preact_grad, preferred_element_type=jnp.float32)
     down_block = jnp.einsum("std,stj->sdj", cotangent, hidden, preferred_element_type=jnp.float32)
     jacobian = jnp.stack([up_block, down_block], axis=1).astype(jnp.bfloat16)
-    grouped = lax.all_to_all(jacobian, "param", split_axis=3, concat_axis=0, tiled=True)
+    ways, here = (lax.axis_size("param"), lax.axis_index("param"))
+    width = jacobian.shape[3] // ways
+    turned = jnp.roll(jacobian, -here * width, axis=3)
+    got = [lax.slice_in_dim(turned, 0, width, axis=3)]
+    for far in range(1, ways):
+        sent = lax.slice_in_dim(turned, far * width, (far + 1) * width, axis=3)
+        got.append(lax.ppermute(sent, "param", [(d, (d + far) % ways) for d in range(ways)]))
+    line = jnp.concatenate(got[::-1], axis=0)
+    grouped = jnp.roll(line, (here + 1) * got[0].shape[0], axis=0)
     chosen_raw = lax.all_to_all(grouped, "chain", split_axis=2, concat_axis=0, tiled=True)
     centred = center_rows(chosen_raw, total)
     gram = lax.psum(gram_of(centred, total), ("chain", "param"))

time: 421 us -> 364 us (0.86); the launches traced: 413 us -> 364 us
  blocking collectives: 150 us -> 96.4 us
  waiting for transfers between devices: 117 us -> 148 us
  local copies, waits for them, and re-layouts: 46.1 us -> 19.7 us
  starting transfers between devices: 0.04 us -> 19.9 us
  matrix products: 44.6 us -> 27.3 us
    all_to_all x1 -> x0, blocking collectives: 53.2 us -> none  [body(): lax.all_to_all(jacobian, 'param', split_axis=3, concat_axis=0, tiled=True)]
    ppermute x0 -> x7, waiting for transfers between devices: none -> 30.1 us  [body(): lax.ppermute(sent, 'param', [(d, (d + far) % ways) for d in range(ways)])]
    all_to_all x4 -> x0, local copies, waits for them, and re-layouts: 20.6 us -> none  [the longest x3 15.7 us: body(): lax.all_to_all(jacobian, 'param', split_axis=3, concat_axis=0, tiled=True)]
    ppermute x0 -> x7, starting transfers between devices: none -> 19.8 us  [body(): lax.ppermute(sent, 'param', [(d, (d + far) % ways) for d in range(ways)])]
    dot_general x1, matrix products: 17.1 us -> 7.26 us  [gram_of(): lax.dot_general(flat, flat, (((1,), (1,)), ((), ())), precision=lax.Preci...]
    div x1, local copies, waits for them, and re-layouts: 10.4 us -> 1.45 us  [center_rows(): return (jac_wide - jnp.mean(jac_wide, axis=0)) / math.sqrt(total)]
    another operation x1 -> x0, local copies, waits for them, and re-layouts: 7.85 us -> none  [body(): jacobian = jnp.stack([up_block, down_block], axis=1).astype(jnp.bfloat16)]
    dot_general x1, matrix products: 12.5 us -> 6.38 us  [body(): lax.dot_general(sample_weights, centred, (((0,), (0,)), ((), ())), precis...]
  transfers between devices with their start and end apart: 1 -> 8, of which waited for: 1 -> 3; matrix products, arithmetic and copies ran while one was open for 0% -> 1% of each run, Pallas kernels for 0% -> 0%
where the time goes in v1:
time: 364 us
  waiting for transfers between devices  148 us (41%)
  blocking collectives  96.4 us (26%)
  other arithmetic  35.8 us (10%)
  matrix products  27.3 us (8%)
  starting transfers between devices  19.9 us (5%)
  local copies, waits for them, and re-layouts  19.7 us (5%)
  between operations  16.5 us (5%)
    psum x1, waiting for transfers between devices, body(): gram = lax.psum(gram_of(centred, total), ('chain', 'param'))  118 us
    all_to_all x1, blocking collectives, body(): lax.all_to_all(grouped, 'chain', split_axis=2, concat_axis=0, tiled=True)  96.4 us
    ppermute x7, waiting for transfers between devices, body(): lax.ppermute(sent, 'param', [(d, (d + far) % ways) for d in range(ways)])  30.1 us
    ppermute x7, starting transfers between devices, body(): lax.ppermute(sent, 'param', [(d, (d + far) % ways) for d in range(ways)])  19.8 us
    another operation x3, other arithmetic, solve_weights(): lower = jnp.linalg.cholesky(system)  12.6 us
    another operation x2, other arithmetic, solve_weights(): lax.linalg.triangular_solve(lower, middle, left_side=True, lower=True, tr...  10.5 us
    unnamed x39, local copies, waits for them, and re-layouts  9.54 us
  transfers between devices with their start and end apart: 8, of which 3 were waited for; matrix products, arithmetic and copies ran while one was open for 1% of the time, Pallas kernels for 0%

profile of v1, /device:TPU:1, one launch (start us, length us, event | category | flops | bytes accessed | tf_op | source)
XLA Modules:
  0.0 363.5 jit_solution(11498926575978030652)
XLA Ops:
  7.2 0.8 add_convert_fusion
  8.1 1.5 multiply_reduce_fusion
  9.5 0.3 copy.52
  9.9 1.0 copy.51
  11.0 0.2 multiply_reduce_fusion.2
  11.2 0.4 convolution_convert_fusion
  11.6 0.5 fusion.16
  12.2 0.4 fusion.49
  12.7 0.8 fusion.22
  13.5 1.7 fusion.15
  15.2 0.2 copy-done.3
  15.4 3.1 convert_bitcast_fusion.1
  18.5 6.5 %convert_bitcast_fusion.2 = bf16[4,1,256,1024]{3,2,0,1:T(8,128)(2,1)} fusion(f32[4,256,1024]{2,1,0:T(8,128)} %copy-done.3, bf16[4,256,256]{1,2,0:T(8,128)(2,1)S(1)} %fusion.15, bf16[1024,256]{1,0:T(8,128)(2,1)S(1)} %copy-done.10, f32[4,256,256]{1,2,0:T(8,128)S(1)} %get-tuple-element.13, f32[4,256]{1,0:T(4,128)S(1)} %add_rsqrt_fusion, ...), kind=kOutput, calls=%fused_computation.23 | convolution fusion | flops 1096548352 | bytes 8396800 | tf_op jit(solution)/shard_map/sti,stj->sij/dot_general | solution.py:89
  25.0 3.8 %fusion.11 = bf16[4,2,256,1024]{3,2,0,1:T(8,128)(2,1)S(1)} fusion(s32[]{:T(128)S(6)} %select_n.33, bf16[4,1,256,1024]{3,2,0,1:T(8,128)(2,1)} %convert_bitcast_fusion.2, bf16[4,1,256,1024]{3,2,0,1:T(8,128)(2,1)} %convert_bitcast_fusion.1), kind=kLoop, calls=%fused_computation.18 | loop fusion | flops 16777216 | bytes 8388612 | tf_op jit(solution)/shard_map/jit(_roll_dynamic)/concatenate | solution.py:94
  28.9 1.9 copy-done.2
  30.8 2.3 fusion.48
  33.2 3.6 collective-permute-start.1
  36.8 1.3 collective-permute-start.2
  38.1 1.3 collective-permute-start.3
  39.4 9.3 %collective-permute-done = bf16[4,2,256,128]{3,2,0,1:T(8,128)(2,1)S(1)} collective-permute-done((bf16[4,2,256,128]{3,2,0,1:T(8,128)(2,1)}, bf16[4,2,256,128]{3,2,0,1:T(8,128)(2,1)S(1)}, u32[]{:S(2)}, u32[]{:S(2)}) %collective-permute-start) | collective-permute-done | bytes 524320 | tf_op jit(solution)/shard_map/ppermute | solution.py:98
  48.7 1.8 collective-permute-start.5
  50.5 11.8 %collective-permute-start.6 = (bf16[4,2,256,128]{3,2,0,1:T(8,128)(2,1)}, bf16[4,2,256,128]{3,2,0,1:T(8,128)(2,1)S(1)}, u32[]{:S(2)}, u32[]{:S(2)}) collective-permute-start(bf16[4,2,256,128]{3,2,0,1:T(8,128)(2,1)} %get-tuple-element.3), channel_id=1, source_target_pairs={{0,1},{1,2},{2,3},{3,4},{4,5},{5,6},{6,7},{7,0},{8,9},{9,10},{10,1... | collective-permute-start | bytes 1572872 | tf_op jit(solution)/shard_map/ppermute | solution.py:98
  62.5 20.8 %collective-permute-done.4 = bf16[4,2,256,128]{3,2,0,1:T(8,128)(2,1)} collective-permute-done((bf16[4,2,256,128]{3,2,0,1:T(8,128)(2,1)}, bf16[4,2,256,128]{3,2,0,1:T(8,128)(2,1)}, u32[]{:S(2)}, u32[]{:S(2)}) %collective-permute-start.4) | collective-permute-done | bytes 524320 | tf_op jit(solution)/shard_map/ppermute | solution.py:98
  83.3 1.1 constant_dynamic-update-slice_fusion.9
  84.6 1.1 slice_dynamic-update-slice_fusion
  86.1 1.1 constant_dynamic-update-slice_fusion.2
  87.3 1.1 slice_dynamic-update-slice_fusion.1
  88.5 0.5 constant_dynamic-slice_fusion
  89.0 2.7 copy.62
  91.7 96.4 %all_to_all.4 = bf16[32,2,256,128]{3,0,1,2:T(8,128)(2,1)S(1)} all-to-all(bf16[32,2,256,128]{3,0,1,2:T(8,128)(2,1)S(1)} %copy.62), channel_id=1, replica_groups=mesh['chain'=4,'param'=8] {'chain'}, dimensions={2} | all-to-all | bytes 8388608 | tf_op jit(solution)/shard_map/all_to_all | solution.py:101
  188.1 1.1 fusion.1
  189.2 1.3 fusion.2
  190.5 1.4 copy.63
  192.0 3.2 copy-done.1
  195.2 7.3 %convolution_bitcast_fusion = f32[128,128]{1,0:T(8,128)} fusion(f32[128,2,64,128]{3,0,2,1:T(8,128)S(1)} %bitcast.87), kind=kOutput, calls=%fused_computation.32 | convolution fusion | flops 3221225472 | bytes 8454144 | tf_op jit(solution)/shard_map/dot_general | solution.py:33
  202.5 0.6 reduce_sum.80
  203.7 117.9 %all-reduce.2.cloned.1.call-done = f32[128,128]{1,0:T(8,128)} async-done(((f32[128,128]{1,0:T(8,128)}), f32[128,128]{1,0:T(8,128)}) %all-reduce.2.cloned.1.call-update) | async-done | bytes 65552 | tf_op jit(solution)/shard_map/psum | solution.py:103
  321.6 1.5 select_reduce_fusion.1
  324.4 0.9 select_add_fusion
  325.4 0.9 fusion.33
  326.2 11.9 %cholesky.13 = f32[128,128]{1,0:T(8,128)S(1)} custom-call(f32[128,128]{1,0:T(8,128)S(1)} %fusion.33), custom_call_target="Cholesky" | custom-call | tf_op jit(solution)/shard_map/jit(cholesky)/cholesky | solution.py:45
  338.2 0.6 compare_reduce_fusion
  338.8 0.7 fusion.30
  339.5 9.8 %custom-call.8 = f32[1,128,128]{1,2,0:T(8,128)S(1)} custom-call(f32[1,128,128]{2,1,0:T(8,128)S(1)} %fusion.30), custom_call_target="InvertDiagBlocksLowerTriangular" | custom-call | tf_op jit(solution)/shard_map/triangular_solve | solution.py:49
  349.3 0.2 convolution_bitcast_fusion.2
  349.5 0.2 fusion.17
  349.7 6.4 %fusion.34 = f32[1,2,64,128]{3,0,2,1:T(1,128)S(1)} fusion(f32[128,2,64,128]{3,0,2,1:T(8,128)} %bitcast.88, f32[128]{0:T(128)S(1)} %fusion.17), kind=kOutput, calls=%fused_computation.89 | convolution fusion | flops 25165824 | bytes 8454656 | tf_op jit(solution)/shard_map/dot_general | solution.py:105
  356.1 0.6 slice_bitcast_fusion
  (53 shorter events, 1.5 us)
Async XLA Ops:
  7.2 4.4 %copy-start = (bf16[8,256,256]{2,1,0:T(8,128)(2,1)S(1)}, bf16[8,256,256]{2,1,0:T(8,128)(2,1)}, u32[]{:S(2)}) copy-start(bf16[8,256,256]{2,1,0:T(8,128)(2,1)} %param.15) | copy-start | bytes 3145732
  7.2 4.0 %copy-start.6 = (bf16[256,256]{1,0:T(8,128)(2,1)S(1)}, bf16[256,256]{1,0:T(8,128)(2,1)}, u32[]{:S(2)}) copy-start(bf16[256,256]{1,0:T(8,128)(2,1)} %param.14) | copy-start | bytes 393220
  7.2 314.5 %all-reduce.2.cloned.1.call-start = ((), (), s32[]{:S(2)}) async-start(), calls=%async_computation.1 | async-start | bytes 131072 | tf_op jit(solution)/shard_map/psum | solution.py:103
  9.9 2.3 copy-start.5
  11.2 1.4 copy-start.4
  12.1 1.3 copy-start.9
  12.1 1.3 copy-start.11
  13.5 1.9 copy-start.3
  15.4 3.1 copy-start.10
  28.9 1.9 copy-start.2
  33.1 15.6 %collective-permute-start = (bf16[4,2,256,128]{3,2,0,1:T(8,128)(2,1)}, bf16[4,2,256,128]{3,2,0,1:T(8,128)(2,1)S(1)}, u32[]{:S(2)}, u32[]{:S(2)}) collective-permute-start(bf16[4,2,256,128]{3,2,0,1:T(8,128)(2,1)} %get-tuple-element.9), channel_id=1, source_target_pairs={{0,7},{1,0},{2,1},{3,2},{4,3},{5,4},{6,5},{7,6},{8,15},{9,8},{10,9... | collective-permute-start | bytes 1572872 | tf_op jit(solution)/shard_map/ppermute | solution.py:98
  33.2 17.3 %collective-permute-start.1 = (bf16[4,2,256,128]{3,2,0,1:T(8,128)(2,1)}, bf16[4,2,256,128]{3,2,0,1:T(8,128)(2,1)S(1)}, u32[]{:S(2)}, u32[]{:S(2)}) collective-permute-start(bf16[4,2,256,128]{3,2,0,1:T(8,128)(2,1)} %get-tuple-element.8), channel_id=1, source_target_pairs={{0,6},{1,7},{2,0},{3,1},{4,2},{5,3},{6,4},{7,5},{8,14},{9,15},{10,... | collective-permute-start | bytes 1572872 | tf_op jit(solution)/shard_map/ppermute | solution.py:98
  36.8 25.6 %collective-permute-start.2 = (bf16[4,2,256,128]{3,2,0,1:T(8,128)(2,1)}, bf16[4,2,256,128]{3,2,0,1:T(8,128)(2,1)S(1)}, u32[]{:S(2)}, u32[]{:S(2)}) collective-permute-start(bf16[4,2,256,128]{3,2,0,1:T(8,128)(2,1)} %get-tuple-element.7), channel_id=1, source_target_pairs={{0,5},{1,6},{2,7},{3,0},{4,1},{5,2},{6,3},{7,4},{8,13},{9,14},{10,... | collective-permute-start | bytes 1572872 | tf_op jit(solution)/shard_map/ppermute | solution.py:98
  38.1 24.4 %collective-permute-start.3 = (bf16[4,2,256,128]{3,2,0,1:T(8,128)(2,1)}, bf16[4,2,256,128]{3,2,0,1:T(8,128)(2,1)S(1)}, u32[]{:S(2)}, u32[]{:S(2)}) collective-permute-start(bf16[4,2,256,128]{3,2,0,1:T(8,128)(2,1)} %get-tuple-element.6), channel_id=1, source_target_pairs={{0,4},{1,5},{2,6},{3,7},{4,0},{5,1},{6,2},{7,3},{8,12},{9,13},{10,... | collective-permute-start | bytes 1572872 | tf_op jit(solution)/shard_map/ppermute | solution.py:98
  39.4 44.0 %collective-permute-start.4 = (bf16[4,2,256,128]{3,2,0,1:T(8,128)(2,1)}, bf16[4,2,256,128]{3,2,0,1:T(8,128)(2,1)}, u32[]{:S(2)}, u32[]{:S(2)}) collective-permute-start(bf16[4,2,256,128]{3,2,0,1:T(8,128)(2,1)} %get-tuple-element.5), channel_id=1, source_target_pairs={{0,3},{1,4},{2,5},{3,6},{4,7},{5,0},{6,1},{7,2},{8,11},{9,12},{10,... | collective-permute-start | bytes 1572872 | tf_op jit(solution)/shard_map/ppermute | solution.py:98
  48.7 35.8 %collective-permute-start.5 = (bf16[4,2,256,128]{3,2,0,1:T(8,128)(2,1)}, bf16[4,2,256,128]{3,2,0,1:T(8,128)(2,1)S(1)}, u32[]{:S(2)}, u32[]{:S(2)}) collective-permute-start(bf16[4,2,256,128]{3,2,0,1:T(8,128)(2,1)} %get-tuple-element.4), channel_id=1, source_target_pairs={{0,2},{1,3},{2,4},{3,5},{4,6},{5,7},{6,0},{7,1},{8,10},{9,11},{10,... | collective-permute-start | bytes 1572872 | tf_op jit(solution)/shard_map/ppermute | solution.py:98
  50.5 34.0 %collective-permute-start.6 = (bf16[4,2,256,128]{3,2,0,1:T(8,128)(2,1)}, bf16[4,2,256,128]{3,2,0,1:T(8,128)(2,1)S(1)}, u32[]{:S(2)}, u32[]{:S(2)}) collective-permute-start(bf16[4,2,256,128]{3,2,0,1:T(8,128)(2,1)} %get-tuple-element.3), channel_id=1, source_target_pairs={{0,1},{1,2},{2,3},{3,4},{4,5},{5,6},{6,7},{7,0},{8,9},{9,10},{10,1... | collective-permute-start | bytes 1572872 | tf_op jit(solution)/shard_map/ppermute | solution.py:98
  192.0 3.2 copy-start.1
  195.2 7.3 %copy-start.8 = (f32[128]{0:T(128)S(1)}, f32[128]{0:T(128)}, u32[]{:S(2)}) copy-start(f32[128]{0:T(128)} %param.11) | copy-start | bytes 1540
  349.7 6.4 %copy-start.7 = (f32[128]{0:T(128)}, f32[128]{0:T(128)S(1)}, u32[]{:S(2)}) copy-start(f32[128]{0:T(128)S(1)} %fusion.17) | copy-start | bytes 1540
Sparse Core Ops, SparseCore 0:
  202.6 119.0 all-reduce.1
